TPU v7x, 256 devices: a whole 4x4x8 slice. The times are simulated.
256 devices in a mesh: layer: 8 (over z), plane: 32 (over y, x, core).
Axes of the slice: x: 4, y: 4, z: 8, core: 2. Of those that a mesh axis runs over, the one named last changes fastest.
Arguments:
- leaf_rhs: bfloat16 [2048, 128, 512], P(('layer', 'plane')), may hold values from -6 to 6
- leaf_inverse: bfloat16 [2048, 128, 128], P(('layer', 'plane')), may hold values from -0.5 to 0.5
- leaf_couple: bfloat16 [2048, 3, 1024, 128], P(('layer', 'plane')), may hold values from -0.09375 to 0.09375
- couple_mask: int32 [2048, 3], P(('layer', 'plane')), may hold values 0 or 1
- leaf_diag: float32 [2048, 128], P(('layer', 'plane')), may hold values from 0.5 to 2
- sep_rhs: bfloat16 [7, 1024, 512], P(None, 'plane'), may hold values from -6 to 6
- sep_inverse: bfloat16 [7, 1024, 1024], P(None, 'plane'), may hold values from -0.1875 to 0.1875
- sep_couple: bfloat16 [7, 2, 1024, 1024], P(None, None, 'plane'), may hold values from -0.125 to 0.125
- sep_diag: float32 [7, 1024], P(None, 'plane'), may hold values from 0.5 to 2
Outputs:
- leaf_solution: bfloat16 [2048, 128, 512], P(('layer', 'plane'))
- sep_solution: bfloat16 [8, 3, 1024, 512], P('layer', None, 'plane')
All inputs are finite; a program needn't handle non-finite values. No bound on the sum of `couple_mask` on one device may be relied on, other than what follows from the above.
Results may differ from a plain program's by a relative error of at most 0.02.
Values may be sent and summed in bfloat16 or wider, within the bound.
A program may use at most 128 MiB of HBM per device.

v0:
```python
import jax
import jax.numpy as jnp
from jax import lax
from jax.sharding import PartitionSpec as P


def from_partner(value, axis, stride):
    mask = 2**stride
    pairs = [(source, source ^ mask) for source in range(lax.axis_size(axis))]
    return lax.ppermute(value, axis, pairs)


def lower_unit(block, first_row):
    row_count = block.shape[-2]
    col_count = block.shape[-1]
    row_ids = first_row + lax.broadcasted_iota(jnp.int32, (row_count, col_count), 0)
    col_ids = lax.broadcasted_iota(jnp.int32, (row_count, col_count), 1)
    below = jnp.where(col_ids < row_ids, block, jnp.zeros_like(block))
    return jnp.where(col_ids == row_ids, jnp.ones_like(block), below)


def body(
    leaf_rhs,
    leaf_inverse,
    leaf_couple,
    couple_mask,
    leaf_diag,
    sep_rhs,
    sep_inverse,
    sep_couple,
    sep_diag,
):
    levels = leaf_couple.shape[1]
    layers = lax.axis_size("layer")
    own_rows = sep_rhs.shape[1]
    layer_id = lax.axis_index("layer")
    plane_id = lax.axis_index("plane")
    first_row = plane_id * own_rows
    leaf_lower = lower_unit(leaf_inverse, 0)
    leaf_y = jnp.einsum(
        "bij,bjr->bir", leaf_lower, leaf_rhs, preferred_element_type=jnp.float32
    ).astype(jnp.bfloat16)
    masked = leaf_couple * couple_mask.astype(jnp.bfloat16)[:, :, None, None]
    totals = lax.psum_scatter(
        jnp.einsum("bksc,bcr->skr", masked, leaf_y, preferred_element_type=jnp.float32),
        "plane",
        scatter_dimension=0,
        tiled=True,
    )
    sep_ids = [
        layers - (layers >> level - 1) + jnp.right_shift(layer_id, level)
        for level in range(1, levels + 1)
    ]

    def select_sep(array, level):
        return lax.dynamic_index_in_dim(array, sep_ids[level - 1], 0, keepdims=False)

    inverses = [
        lower_unit(select_sep(sep_inverse, level), first_row) for level in range(1, levels + 1)
    ]
    sep_z = []
    for level in range(1, levels + 1):
        partner = from_partner(totals[:, level - 1 :], "layer", level - 1)
        totals = jnp.concatenate([totals[:, : level - 1], totals[:, level - 1 :] + partner], axis=1)
        residual = (select_sep(sep_rhs, level).astype(jnp.float32) - totals[:, level - 1]).astype(
            jnp.bfloat16
        )
        residual_full = lax.all_gather(residual, "plane", axis=0, tiled=True)
        solved = jnp.dot(
            inverses[level - 1], residual_full, preferred_element_type=jnp.float32
        ).astype(jnp.bfloat16)
        if level < levels:
            solved_full = lax.all_gather(solved, "plane", axis=0, tiled=True)
        if level < levels:
            blocks = select_sep(sep_couple, level)[: levels - level]
            coupling = jnp.einsum(
                "jos,sr->ojr", blocks, solved_full, preferred_element_type=jnp.float32
            )
            totals = jnp.concatenate([totals[:, :level], totals[:, level:] + coupling], axis=1)
        sep_z.append(solved.astype(jnp.float32) / select_sep(sep_diag, level)[:, None])
    answers = [None] * levels
    for level in range(levels, 0, -1):
        if level < levels:
            blocks = select_sep(sep_couple, level)[: levels - level]
            upper_rows = jnp.stack(answers[level:])

            def couple_back(offset_row, row_count, blocks=blocks, upper_rows=upper_rows):
                return jnp.einsum(
                    "jos,jor->sr", blocks, upper_rows, preferred_element_type=jnp.float32
                )

            carried = lax.psum_scatter(
                couple_back(jnp.int32(0), lax.axis_size("plane") * own_rows),
                "plane",
                scatter_dimension=0,
                tiled=True,
            )
            target_now = (sep_z[level - 1] - carried).astype(jnp.bfloat16)
        else:
            target_now = sep_z[level - 1].astype(jnp.bfloat16)
        lower_part = inverses[level - 1]

        def transpose_solve(offset_row, row_count, lower_part=lower_part, target_now=target_now):
            return lax.dot_general(
                lower_part, target_now, (((0,), (0,)), ((), ())), preferred_element_type=jnp.float32
            )

        answers[level - 1] = lax.psum_scatter(
            transpose_solve(jnp.int32(0), lax.axis_size("plane") * own_rows),
            "plane",
            scatter_dimension=0,
            tiled=True,
        ).astype(jnp.bfloat16)
    above = lax.all_gather(jnp.stack(answers), "plane", axis=1, tiled=True)
    back_terms = jnp.einsum("bksc,ksr->bcr", masked, above, preferred_element_type=jnp.float32)
    leaf_target = (leaf_y.astype(jnp.float32) / leaf_diag[:, :, None] - back_terms).astype(
        jnp.bfloat16
    )
    leaf_solution = jnp.einsum(
        "bjc,bjr->bcr", leaf_lower, leaf_target, preferred_element_type=jnp.float32
    ).astype(jnp.bfloat16)
    sep_solution = jnp.stack(answers)[None]
    return (leaf_solution, sep_solution)


def solution(mesh):
    in_specs = (
        P(("layer", "plane"), None, None),
        P(("layer", "plane"), None, None),
        P(("layer", "plane"), None, None, None),
        P(("layer", "plane"), None),
        P(("layer", "plane"), None),
        P(None, "plane", None),
        P(None, "plane", None),
        P(None, None, "plane", None),
        P(None, "plane"),
    )
    out_specs = (P(("layer", "plane"), None, None), P("layer", None, "plane", None))
    return jax.shard_map(body, mesh=mesh, in_specs=in_specs, out_specs=out_specs, check_vma=False)
```

profile of v0, /device:TPU:1, one launch (start us, length us, event | category | flops | bytes accessed | tf_op | source)
XLA Modules:
  0.0 960.2 jit_solution(12969961117015314941)
XLA Ops:
  9.8 8.7 fusion.7
  18.5 9.5 copy.23
  29.8 132.8 %all-reduce.3.cloned.1.call-done = f32[1024,3,512]{2,1,0:T(4,128)} async-done(((f32[1024,3,512]{2,1,0:T(4,128)}), f32[1024,3,512]{2,1,0:T(4,128)}) %all-reduce.3.cloned.1.call-update) | async-done | bytes 6291472
  165.1 4.3 collective-permute-done
  169.4 1.4 fusion.57
  170.9 49.2 %all-gather.7.cloned.1.call-done = bf16[1024,512]{1,0:T(8,128)(2,1)} async-done(((bf16[32,512]{1,0:T(8,128)(2,1)}), bf16[1024,512]{1,0:T(8,128)(2,1)}) %all-gather.7.cloned.1.call-update) | async-done | bytes 1048592 | tf_op jit(solution)/shard_map/all_gather | solution.py:68
  220.1 2.2 convolution_convert_fusion.3
  222.3 48.4 %all-gather.9.cloned.1.call-done = bf16[1024,512]{1,0:T(8,128)(2,1)} async-done(((bf16[32,512]{1,0:T(8,128)(2,1)}), bf16[1024,512]{1,0:T(8,128)(2,1)}) %all-gather.9.cloned.1.call-update) | async-done | bytes 1048592 | tf_op jit(solution)/shard_map/all_gather | solution.py:73
  270.7 1.5 slice_add_fusion
  272.3 2.3 collective-permute-start.1
  274.6 6.3 collective-permute-done.1
  280.9 1.4 fusion.55
  282.4 48.1 %all-gather.11.cloned.1.call-done = bf16[1024,512]{1,0:T(8,128)(2,1)} async-done(((bf16[32,512]{1,0:T(8,128)(2,1)}), bf16[1024,512]{1,0:T(8,128)(2,1)}) %all-gather.11.cloned.1.call-update) | async-done | bytes 1048592 | tf_op jit(solution)/shard_map/all_gather | solution.py:68
  330.5 2.2 convolution_convert_fusion.2
  332.7 48.3 %all-gather.13.cloned.1.call-done = bf16[1024,512]{1,0:T(8,128)(2,1)} async-done(((bf16[32,512]{1,0:T(8,128)(2,1)}), bf16[1024,512]{1,0:T(8,128)(2,1)}) %all-gather.13.cloned.1.call-update) | async-done | bytes 1048592 | tf_op jit(solution)/shard_map/all_gather | solution.py:73
  381.0 1.5 slice_add_fusion.1
  382.5 5.5 collective-permute-start.2
  388.0 2.1 collective-permute-done.2
  390.1 1.4 fusion.61
  392.4 48.5 %all-gather.15.cloned.1.call-done = bf16[1024,512]{1,0:T(8,128)(2,1)} async-done(((bf16[32,512]{1,0:T(8,128)(2,1)}), bf16[1024,512]{1,0:T(8,128)(2,1)}) %all-gather.15.cloned.1.call-update) | async-done | bytes 1048592 | tf_op jit(solution)/shard_map/all_gather | solution.py:68
  440.9 3.3 fusion.28
  444.3 84.7 %reduce-scatter.6.cloned.1.call-done = f32[32,512]{1,0:T(8,128)} async-done(((f32[1024,512]{1,0:T(8,128)}), f32[32,512]{1,0:T(8,128)}) %reduce-scatter.6.cloned.1.call-update) | async-done | bytes 65552 | tf_op jit(solution)/shard_map/reduce_scatter | solution.py:108
  529.0 2.7 fusion.68
  531.8 87.4 %reduce-scatter.8.cloned.1.call-done = f32[32,512]{1,0:T(8,128)} async-done(((f32[1024,512]{1,0:T(8,128)}), f32[32,512]{1,0:T(8,128)}) %reduce-scatter.8.cloned.1.call-update) | async-done | bytes 65552 | tf_op jit(solution)/shard_map/reduce_scatter | solution.py:92
  619.2 2.7 fusion.69
  622.0 87.4 %reduce-scatter.10.cloned.1.call-done = f32[32,512]{1,0:T(8,128)} async-done(((f32[1024,512]{1,0:T(8,128)}), f32[32,512]{1,0:T(8,128)}) %reduce-scatter.10.cloned.1.call-update) | async-done | bytes 65552 | tf_op jit(solution)/shard_map/reduce_scatter | solution.py:108
  710.3 2.7 convolution_bitcast_fusion
  713.1 86.4 %reduce-scatter.12.cloned.1.call-done = f32[32,512]{1,0:T(8,128)} async-done(((f32[1024,512]{1,0:T(8,128)}), f32[32,512]{1,0:T(8,128)}) %reduce-scatter.12.cloned.1.call-update) | async-done | bytes 65552 | tf_op jit(solution)/shard_map/reduce_scatter | solution.py:92
  799.5 2.7 fusion.70
  802.3 87.4 %reduce-scatter.14.cloned.1.call-done = f32[32,512]{1,0:T(8,128)} async-done(((f32[1024,512]{1,0:T(8,128)}), f32[32,512]{1,0:T(8,128)}) %reduce-scatter.14.cloned.1.call-update) | async-done | bytes 65552 | tf_op jit(solution)/shard_map/reduce_scatter | solution.py:108
  891.3 53.4 %all-gather.17.cloned.1.call-done = bf16[3,1024,512]{2,1,0:T(8,128)(2,1)} async-done(((bf16[3,32,512]{2,1,0:T(8,128)(2,1)}), bf16[3,1024,512]{2,1,0:T(8,128)(2,1)}) %all-gather.17.cloned.1.call-update) | async-done | bytes 3145744 | tf_op jit(solution)/shard_map/all_gather | solution.py:114
  944.8 8.6 fusion.20
  (56 shorter events, 10.2 us)
Async XLA Ops:
  7.2 1.2 copy-start
  7.2 155.5 %all-reduce.3.cloned.1.call-start = ((), (), s32[]{:S(2)}) async-start(), calls=%async_computation.16 | async-start | bytes 16777216
  27.9 0.7 copy-start.7
  27.9 192.1 %copy-start.1 = (bf16[7,32,1024]{2,1,0:T(8,128)(2,1)S(1)}, bf16[7,32,1024]{2,1,0:T(8,128)(2,1)}, u32[]{:S(2)}) copy-start(bf16[7,32,1024]{2,1,0:T(8,128)(2,1)} %param.15) | copy-start | bytes 1376260
  28.0 192.1 %all-gather.7.cloned.1.call-start = ((), (), s32[]{:S(2)}) async-start(), calls=%async_computation.5 | async-start | bytes 1081344 | tf_op jit(solution)/shard_map/all_gather | solution.py:68
  163.7 5.6 collective-permute-start
  170.8 99.9 %all-gather.9.cloned.1.call-start = ((), (), s32[]{:S(2)}) async-start(), calls=%async_computation.6 | async-start | bytes 1081344 | tf_op jit(solution)/shard_map/all_gather | solution.py:73
  222.2 108.2 %all-gather.11.cloned.1.call-start = ((), (), s32[]{:S(2)}) async-start(), calls=%async_computation.7 | async-start | bytes 1081344 | tf_op jit(solution)/shard_map/all_gather | solution.py:68
  272.3 8.7 collective-permute-start.1
  282.4 98.7 %all-gather.13.cloned.1.call-start = ((), (), s32[]{:S(2)}) async-start(), calls=%async_computation.8 | async-start | bytes 1081344 | tf_op jit(solution)/shard_map/all_gather | solution.py:73
  332.7 108.2 %all-gather.15.cloned.1.call-start = ((), (), s32[]{:S(2)}) async-start(), calls=%async_computation.9 | async-start | bytes 1081344 | tf_op jit(solution)/shard_map/all_gather | solution.py:68
  382.5 7.6 collective-permute-start.2
  391.6 137.5 %reduce-scatter.6.cloned.1.call-start = ((), (), s32[]{:S(2)}) async-start(), calls=%async_computation.10 | async-start | bytes 2162688 | tf_op jit(solution)/shard_map/reduce_scatter | solution.py:108
  444.2 175.0 %copy-start.3 = (bf16[32,512]{1,0:T(8,128)(2,1)S(1)}, bf16[32,512]{1,0:T(8,128)(2,1)}, u32[]{:S(2)}) copy-start(bf16[32,512]{1,0:T(8,128)(2,1)} %convolution_convert_fusion.2) | copy-start | bytes 98308
  444.2 175.0 %reduce-scatter.8.cloned.1.call-start = ((), (), s32[]{:S(2)}) async-start(), calls=%async_computation.11 | async-start | bytes 2162688 | tf_op jit(solution)/shard_map/reduce_scatter | solution.py:92
  531.7 90.3 %copy-start.5 = (f32[32,512]{1,0:T(8,128)S(1)}, f32[32,512]{1,0:T(8,128)}, u32[]{:S(2)}) copy-start(f32[32,512]{1,0:T(8,128)} %reduce-scatter.6.cloned.1.call-done) | copy-start | bytes 196612
  531.7 177.7 %reduce-scatter.10.cloned.1.call-start = ((), (), s32[]{:S(2)}) async-start(), calls=%async_computation.12 | async-start | bytes 2162688 | tf_op jit(solution)/shard_map/reduce_scatter | solution.py:108
  621.9 177.6 %copy-start.2 = (bf16[32,512]{1,0:T(8,128)(2,1)S(1)}, bf16[32,512]{1,0:T(8,128)(2,1)}, u32[]{:S(2)}) copy-start(bf16[32,512]{1,0:T(8,128)(2,1)} %convolution_convert_fusion.3) | copy-start | bytes 98308
  622.0 177.6 %reduce-scatter.12.cloned.1.call-start = ((), (), s32[]{:S(2)}) async-start(), calls=%async_computation.13 | async-start | bytes 2162688 | tf_op jit(solution)/shard_map/reduce_scatter | solution.py:92
  713.0 231.7 %copy-start.4 = (bf16[8,128,128]{2,1,0:T(8,128)(2,1)S(1)}, bf16[8,128,128]{2,1,0:T(8,128)(2,1)}, u32[]{:S(2)}) copy-start(bf16[8,128,128]{2,1,0:T(8,128)(2,1)} %param.10) | copy-start | bytes 786436
  713.0 231.7 %copy-start.6 = (f32[8,128]{1,0:T(8,128)S(1)}, f32[8,128]{1,0:T(8,128)}, u32[]{:S(2)}) copy-start(f32[8,128]{1,0:T(8,128)} %param.13) | copy-start | bytes 12292
  713.1 176.7 %reduce-scatter.14.cloned.1.call-start = ((), (), s32[]{:S(2)}) async-start(), calls=%async_computation.14 | async-start | bytes 2162688 | tf_op jit(solution)/shard_map/reduce_scatter | solution.py:108
  802.3 142.5 %all-gather.17.cloned.1.call-start = ((), (), s32[]{:S(2)}) async-start(), calls=%async_computation.15 | async-start | bytes 3244032 | tf_op jit(solution)/shard_map/all_gather | solution.py:114
Sparse Core Ops, SparseCore 0:
  28.1 134.5 all-reduce.2
  171.0 49.0 all-gather.6
  223.5 47.1 all-gather.8
  282.5 47.9 all-gather.10
  333.8 47.1 all-gather.12
  391.7 49.1 all-gather.14
  445.2 83.7 reduce-scatter.5
  533.3 85.8 reduce-scatter.7
  623.5 85.8 reduce-scatter.9
  713.6 85.8 reduce-scatter.11
  803.9 85.8 reduce-scatter.13
  893.1 51.5 all-gather.16
where the time goes:
time: 961 us; the launch traced here: 960 us
  waiting for transfers between devices  875 us (91%)
  matrix products  40.2 us (4%)
  between operations  15 us (2%)
  local copies, waits for them, and re-layouts  12.9 us (1%)
  starting transfers between devices  9.71 us (1%)
    reduce_scatter x3, waiting for transfers between devices, body(): lax.psum_scatter(transpose_solve(jnp.int32(0), lax.axis_size('plane') * o...  260 us
    reduce_scatter x2, waiting for transfers between devices, body(): lax.psum_scatter(couple_back(jnp.int32(0), lax.axis_size('plane') * own_r...  174 us
    all_gather x3, waiting for transfers between devices, body(): residual_full = lax.all_gather(residual, 'plane', axis=0, tiled=True)  146 us
    unnamed x13, waiting for transfers between devices  133 us
    all_gather x2, waiting for transfers between devices, body(): solved_full = lax.all_gather(solved, 'plane', axis=0, tiled=True)  96.7 us
    all_gather x1, waiting for transfers between devices, body(): above = lax.all_gather(jnp.stack(answers), 'plane', axis=1, tiled=True)  53.4 us
  transfers between devices with their start and end apart: 15, of which 15 were waited for; matrix products, arithmetic and copies ran while one was open for 0% of the time, Pallas kernels for 0%

commit v1 on v0

--- a/solution.py
+++ b/solution.py
@@ -111,7 +111,11 @@
             scatter_dimension=0,
             tiled=True,
         ).astype(jnp.bfloat16)
-    above = lax.all_gather(jnp.stack(answers), "plane", axis=1, tiled=True)
+    part = jnp.stack(answers)
+    size = lax.axis_size("plane")
+    parts = jnp.stack([part for _ in range(size)])
+    parts = lax.all_to_all(parts, "plane", split_axis=0, concat_axis=0)
+    above = jnp.concatenate(parts, axis=1)
     back_terms = jnp.einsum("bksc,ksr->bcr", masked, above, preferred_element_type=jnp.float32)
     leaf_target = (leaf_y.astype(jnp.float32) / leaf_diag[:, :, None] - back_terms).astype(
         jnp.bfloat16

time: 961 us -> 957 us (level)
  waiting for transfers between devices: 875 us -> 822 us
  blocking collectives: 0 us -> 46.8 us
    all_gather x1 -> x0, waiting for transfers between devices: 53.4 us -> none  [body(): above = lax.all_gather(jnp.stack(answers), 'plane', axis=1, tiled=True)]
    all_to_all x0 -> x1, blocking collectives: none -> 46.8 us  [body(): parts = lax.all_to_all(parts, 'plane', split_axis=0, concat_axis=0)]
    unnamed x13 -> x12, waiting for transfers between devices: 133 us -> 133 us
  transfers between devices with their start and end apart: 15 -> 14, of which waited for: 15 -> 14; matrix products, arithmetic and copies ran while one was open for 0% -> 0% of each run, Pallas kernels for 0% -> 0%
where the time goes in v1:
time: 957 us; the launch traced here: 956 us
  waiting for transfers between devices  822 us (86%)
  blocking collectives  46.8 us (5%)
  matrix products  40.1 us (4%)
  local copies, waits for them, and re-layouts  15.4 us (2%)
  between operations  14.6 us (2%)
  starting transfers between devices  9.67 us (1%)
    reduce_scatter x3, waiting for transfers between devices, body(): lax.psum_scatter(transpose_solve(jnp.int32(0), lax.axis_size('plane') * o...  260 us
    reduce_scatter x2, waiting for transfers between devices, body(): lax.psum_scatter(couple_back(jnp.int32(0), lax.axis_size('plane') * own_r...  174 us
    all_gather x3, waiting for transfers between devices, body(): residual_full = lax.all_gather(residual, 'plane', axis=0, tiled=True)  146 us
    unnamed x12, waiting for transfers between devices  133 us
    all_gather x2, waiting for transfers between devices, body(): solved_full = lax.all_gather(solved, 'plane', axis=0, tiled=True)  96.7 us
    all_to_all x1, blocking collectives, body(): parts = lax.all_to_all(parts, 'plane', split_axis=0, concat_axis=0)  46.8 us
  transfers between devices with their start and end apart: 14, of which 14 were waited for; matrix products, arithmetic and copies ran while one was open for 0% of the time, Pallas kernels for 0%

profile of v1, /device:TPU:1, one launch (start us, length us, event | category | flops | bytes accessed | tf_op | source)
XLA Modules:
  0.0 955.6 jit_solution(9984068140575591758)
XLA Ops:
  9.8 8.7 fusion.6
  18.4 9.5 copy.32
  29.8 132.8 %all-reduce.3.cloned.1.call-done = f32[1024,3,512]{2,1,0:T(4,128)} async-done(((f32[1024,3,512]{2,1,0:T(4,128)}), f32[1024,3,512]{2,1,0:T(4,128)}) %all-reduce.3.cloned.1.call-update) | async-done | bytes 6291472
  165.1 4.3 collective-permute-done
  169.4 1.4 fusion.50
  170.9 49.2 %all-gather.6.cloned.1.call-done = bf16[1024,512]{1,0:T(8,128)(2,1)} async-done(((bf16[32,512]{1,0:T(8,128)(2,1)}), bf16[1024,512]{1,0:T(8,128)(2,1)}) %all-gather.6.cloned.1.call-update) | async-done | bytes 1048592 | tf_op jit(solution)/shard_map/all_gather | solution.py:68
  220.0 2.2 convolution_convert_fusion.3
  222.3 48.4 %all-gather.8.cloned.1.call-done = bf16[1024,512]{1,0:T(8,128)(2,1)} async-done(((bf16[32,512]{1,0:T(8,128)(2,1)}), bf16[1024,512]{1,0:T(8,128)(2,1)}) %all-gather.8.cloned.1.call-update) | async-done | bytes 1048592 | tf_op jit(solution)/shard_map/all_gather | solution.py:73
  270.7 1.5 slice_add_fusion
  272.2 2.4 collective-permute-start.1
  274.6 6.3 collective-permute-done.1
  280.9 1.4 fusion.48
  282.4 48.1 %all-gather.10.cloned.1.call-done = bf16[1024,512]{1,0:T(8,128)(2,1)} async-done(((bf16[32,512]{1,0:T(8,128)(2,1)}), bf16[1024,512]{1,0:T(8,128)(2,1)}) %all-gather.10.cloned.1.call-update) | async-done | bytes 1048592 | tf_op jit(solution)/shard_map/all_gather | solution.py:68
  330.5 2.2 convolution_convert_fusion.2
  332.7 48.3 %all-gather.12.cloned.1.call-done = bf16[1024,512]{1,0:T(8,128)(2,1)} async-done(((bf16[32,512]{1,0:T(8,128)(2,1)}), bf16[1024,512]{1,0:T(8,128)(2,1)}) %all-gather.12.cloned.1.call-update) | async-done | bytes 1048592 | tf_op jit(solution)/shard_map/all_gather | solution.py:73
  381.0 1.5 slice_add_fusion.1
  382.5 5.5 collective-permute-start.2
  388.0 2.1 collective-permute-done.2
  392.4 48.5 %all-gather.14.cloned.1.call-done = bf16[1024,512]{1,0:T(8,128)(2,1)} async-done(((bf16[32,512]{1,0:T(8,128)(2,1)}), bf16[1024,512]{1,0:T(8,128)(2,1)}) %all-gather.14.cloned.1.call-update) | async-done | bytes 1048592 | tf_op jit(solution)/shard_map/all_gather | solution.py:68
  440.9 3.3 fusion.21
  444.2 84.8 %reduce-scatter.6.cloned.1.call-done = f32[32,512]{1,0:T(8,128)} async-done(((f32[1024,512]{1,0:T(8,128)}), f32[32,512]{1,0:T(8,128)}) %reduce-scatter.6.cloned.1.call-update) | async-done | bytes 65552 | tf_op jit(solution)/shard_map/reduce_scatter | solution.py:108
  529.0 2.7 fusion.61
  531.7 87.5 %reduce-scatter.8.cloned.1.call-done = f32[32,512]{1,0:T(8,128)} async-done(((f32[1024,512]{1,0:T(8,128)}), f32[32,512]{1,0:T(8,128)}) %reduce-scatter.8.cloned.1.call-update) | async-done | bytes 65552 | tf_op jit(solution)/shard_map/reduce_scatter | solution.py:92
  619.2 2.7 fusion.62
  622.0 87.4 %reduce-scatter.10.cloned.1.call-done = f32[32,512]{1,0:T(8,128)} async-done(((f32[1024,512]{1,0:T(8,128)}), f32[32,512]{1,0:T(8,128)}) %reduce-scatter.10.cloned.1.call-update) | async-done | bytes 65552 | tf_op jit(solution)/shard_map/reduce_scatter | solution.py:108
  710.3 2.7 convolution_bitcast_fusion
  713.1 86.5 %reduce-scatter.12.cloned.1.call-done = f32[32,512]{1,0:T(8,128)} async-done(((f32[1024,512]{1,0:T(8,128)}), f32[32,512]{1,0:T(8,128)}) %reduce-scatter.12.cloned.1.call-update) | async-done | bytes 65552 | tf_op jit(solution)/shard_map/reduce_scatter | solution.py:92
  799.5 2.7 fusion.63
  802.2 87.5 %reduce-scatter.14.cloned.1.call-done = f32[32,512]{1,0:T(8,128)} async-done(((f32[1024,512]{1,0:T(8,128)}), f32[32,512]{1,0:T(8,128)}) %reduce-scatter.14.cloned.1.call-update) | async-done | bytes 65552 | tf_op jit(solution)/shard_map/reduce_scatter | solution.py:108
  891.6 46.8 %all_to_all.5 = bf16[32,3,32,512]{3,2,1,0:T(8,128)(2,1)S(1)} all-to-all(bf16[32,3,32,512]{3,2,1,0:T(8,128)(2,1)S(1)} %stack.19), channel_id=1, replica_groups=mesh['layer'=8,'plane'=32] {'plane'}, dimensions={0} | all-to-all | bytes 6291456 | tf_op jit(solution)/shard_map/all_to_all | solution.py:117
  938.4 2.0 copy.35
  940.5 8.6 fusion.15
  (56 shorter events, 11.8 us)
Async XLA Ops:
  7.2 1.2 copy-start
  7.2 155.4 %all-reduce.3.cloned.1.call-start = ((), (), s32[]{:S(2)}) async-start(), calls=%async_computation.16 | async-start | bytes 16777216
  27.9 0.7 copy-start.7
  27.9 192.1 %copy-start.1 = (bf16[7,32,1024]{2,1,0:T(8,128)(2,1)S(1)}, bf16[7,32,1024]{2,1,0:T(8,128)(2,1)}, u32[]{:S(2)}) copy-start(bf16[7,32,1024]{2,1,0:T(8,128)(2,1)} %param.15) | copy-start | bytes 1376260
  27.9 192.1 %all-gather.6.cloned.1.call-start = ((), (), s32[]{:S(2)}) async-start(), calls=%async_computation.6 | async-start | bytes 1081344 | tf_op jit(solution)/shard_map/all_gather | solution.py:68
  163.7 5.6 collective-permute-start
  170.8 99.9 %all-gather.8.cloned.1.call-start = ((), (), s32[]{:S(2)}) async-start(), calls=%async_computation.7 | async-start | bytes 1081344 | tf_op jit(solution)/shard_map/all_gather | solution.py:73
  222.2 108.2 %all-gather.10.cloned.1.call-start = ((), (), s32[]{:S(2)}) async-start(), calls=%async_computation.8 | async-start | bytes 1081344 | tf_op jit(solution)/shard_map/all_gather | solution.py:68
  272.2 8.7 collective-permute-start.1
  282.3 98.7 %all-gather.12.cloned.1.call-start = ((), (), s32[]{:S(2)}) async-start(), calls=%async_computation.9 | async-start | bytes 1081344 | tf_op jit(solution)/shard_map/all_gather | solution.py:73
  332.7 108.2 %all-gather.14.cloned.1.call-start = ((), (), s32[]{:S(2)}) async-start(), calls=%async_computation.10 | async-start | bytes 1081344 | tf_op jit(solution)/shard_map/all_gather | solution.py:68
  382.5 7.6 collective-permute-start.2
  391.5 137.5 %reduce-scatter.6.cloned.1.call-start = ((), (), s32[]{:S(2)}) async-start(), calls=%async_computation.11 | async-start | bytes 2162688 | tf_op jit(solution)/shard_map/reduce_scatter | solution.py:108
  444.2 175.0 %copy-start.3 = (bf16[32,512]{1,0:T(8,128)(2,1)S(1)}, bf16[32,512]{1,0:T(8,128)(2,1)}, u32[]{:S(2)}) copy-start(bf16[32,512]{1,0:T(8,128)(2,1)} %convolution_convert_fusion.2) | copy-start | bytes 98308
  444.2 175.0 %reduce-scatter.8.cloned.1.call-start = ((), (), s32[]{:S(2)}) async-start(), calls=%async_computation.12 | async-start | bytes 2162688 | tf_op jit(solution)/shard_map/reduce_scatter | solution.py:92
  531.7 90.3 %copy-start.5 = (f32[32,512]{1,0:T(8,128)S(1)}, f32[32,512]{1,0:T(8,128)}, u32[]{:S(2)}) copy-start(f32[32,512]{1,0:T(8,128)} %reduce-scatter.6.cloned.1.call-done) | copy-start | bytes 196612
  531.7 177.7 %reduce-scatter.10.cloned.1.call-start = ((), (), s32[]{:S(2)}) async-start(), calls=%async_computation.13 | async-start | bytes 2162688 | tf_op jit(solution)/shard_map/reduce_scatter | solution.py:108
  621.9 177.6 %copy-start.2 = (bf16[32,512]{1,0:T(8,128)(2,1)S(1)}, bf16[32,512]{1,0:T(8,128)(2,1)}, u32[]{:S(2)}) copy-start(bf16[32,512]{1,0:T(8,128)(2,1)} %convolution_convert_fusion.3) | copy-start | bytes 98308
  621.9 177.6 %reduce-scatter.12.cloned.1.call-start = ((), (), s32[]{:S(2)}) async-start(), calls=%async_computation.14 | async-start | bytes 2162688 | tf_op jit(solution)/shard_map/reduce_scatter | solution.py:92
  713.0 176.7 %reduce-scatter.14.cloned.1.call-start = ((), (), s32[]{:S(2)}) async-start(), calls=%async_computation.15 | async-start | bytes 2162688 | tf_op jit(solution)/shard_map/reduce_scatter | solution.py:108
  938.4 2.1 copy-start.4
  938.4 2.1 copy-start.6
Sparse Core Ops, SparseCore 0:
  28.1 134.5 all-reduce.2
  170.9 49.0 all-gather.5
  223.5 47.1 all-gather.7
  282.5 47.9 all-gather.9
  333.8 47.1 all-gather.11
  391.7 49.1 all-gather.13
  445.2 83.7 reduce-scatter.5
  533.3 85.8 reduce-scatter.7
  623.5 85.8 reduce-scatter.9
  713.6 85.8 reduce-scatter.11
  803.8 85.8 reduce-scatter.13
